TPU v7x, 32 devices: a whole 2x2x4 slice. The times are simulated.
32 devices in a mesh: lat: 4 (over x, core), lon: 8 (over z, y).
Axes of the slice: x: 2, y: 2, z: 4, core: 2. Of those that a mesh axis runs over, the one named last changes fastest.
Arguments:
- latent_field: float32 [32, 8, 64, 1024], P(None, None, 'lat', 'lon'), may hold values from -6 to 6
- east_courant: float32 [8, 64, 1024], P(None, 'lat', 'lon'), may hold values from -0.45 to 0.45
- north_courant: float32 [8, 64, 1024], P(None, 'lat', 'lon'), may hold values from -0.45 to 0.45
- mixing: float32 [7, 64, 1024], P(None, 'lat', 'lon'), may hold values from 0.2 to 5
- sunlit: int32 [4, 64], P('lat', 'lon'), may hold values from 0 to 1, as said below
- decode_w: bfloat16 [224, 32], replicated, may hold values from -1 to 1
- react_a: bfloat16 [256, 224], replicated, may hold values from -0.375 to 0.375
- react_b: bfloat16 [256, 224], replicated, may hold values from -0.375 to 0.375
- stoich: bfloat16 [224, 256], replicated, may hold values from -0.375 to 0.375
- encode_w: bfloat16 [32, 224], replicated, may hold values from -0.375 to 0.375
- rate_const: float32 [256], replicated, may hold values from 0.05 to 0.5
Outputs:
- advanced: float32 [32, 8, 64, 1024], P(None, None, 'lat', 'lon')
Inputs may be any that keep to these rules, and one draw needn't show every extreme that they name: In each row of blocks the sunlit blocks form one run, periodic in longitude, of 16 to 48 blocks.
All inputs are finite; a program needn't handle non-finite values.
Results may differ from a plain program's by a relative error of at most 0.0035.
Values may be sent and summed in bfloat16 or wider, within the bound.
No kernel may reach another device: no remote copies, remote signals or barrier semaphores. Data moves between devices by JAX's collectives and lax.ppermute only.
A program may use at most 128 MiB of HBM per device.

v0:
```python
import functools

import jax
import jax.numpy as jnp
from jax import lax
from jax.experimental import pallas as pl
from jax.experimental.pallas import tpu as pltpu
from jax.sharding import PartitionSpec as P

BLOCK = 16
SUBSTEPS = 2
STEPS = 2
GROUP = 16
ROWS_AT_ONCE = 2

F32 = jnp.float32
BF16 = jnp.bfloat16
VMEM_BYTES = 48 * 1024 * 1024


def lane_ids(shape):
    return lax.broadcasted_iota(jnp.int32, shape, len(shape) - 1)


def fold_kernel(decode_t, react_a_t, react_b_t, stoich, encode, rate, linear_out, encode_out):
    n_reactions = react_a_t.shape[1]
    contract = (((0,), (1,)), ((), ()))
    for part, react in enumerate((react_a_t, react_b_t)):
        product = lax.dot_general(
            react[...], decode_t[...], contract, preferred_element_type=F32
        )
        for group in range(n_reactions // GROUP):
            at = (2 * group + part) * GROUP
            linear_out[at : at + GROUP, :] = product[
                group * GROUP : (group + 1) * GROUP
            ].astype(BF16)
    folded = jnp.dot(encode[...], stoich[...], preferred_element_type=F32)
    encode_out[...] = (folded * rate[...]).astype(BF16)


def fold_weights(decode_w, react_a, react_b, stoich, encode_w, rate_const):
    n_reactions, n_species = react_a.shape[0], decode_w.shape[1]
    return pl.pallas_call(
        fold_kernel,
        out_shape=(
            jax.ShapeDtypeStruct((2 * n_reactions, n_species), BF16),
            jax.ShapeDtypeStruct((n_species, n_reactions), BF16),
        ),
        cost_estimate=pl.CostEstimate(flops=20_000_000, bytes_accessed=500_000, transcendentals=0),
        name="fold_weights",
    )(decode_w.T, react_a.T, react_b.T, stoich, encode_w, rate_const[None])


def pack_sides(value, coef, at, west, east):
    lanes = lane_ids(value.shape)
    size = value.shape[-1]
    turned = pltpu.roll(value * coef, at, 1)
    west = jnp.where(lanes == at, turned, west)
    east = jnp.where(lanes == (at + size - 1) % size, turned, east)
    return west, east


def edge_kernel(n_levels, n_rows, latent, east_c, north_c, moved_out, west, east, south, north):
    n_species, n_cols = west.shape
    cells = n_levels * n_rows
    lanes = lane_ids((1, n_cols))

    def row(r, sides):
        for level in range(n_levels):
            at = level * n_rows + r
            value = latent[pl.ds(at, n_species, stride=cells), :]
            moved_out[level, r] = value
            speed = east_c[level, pl.ds(r, 1), :]
            coef = jnp.where(lanes == 0, jnp.minimum(speed, 0.0), jnp.maximum(speed, 0.0))
            sides = pack_sides(value, coef, at, *sides)
        return sides

    zeros = jnp.zeros((n_species, n_cols), F32)
    west[...], east[...] = lax.fori_loop(0, n_rows, row, (zeros, zeros))
    for level in range(n_levels):
        for edge, out, clip in ((0, south, jnp.minimum), (n_rows - 1, north, jnp.maximum)):
            speed = clip(north_c[level, edge : edge + 1, :], 0.0)
            out[level] = (moved_out[level, edge] * speed).astype(BF16)


def step_kernel(
    n_levels,
    n_rows,
    last,
    sun,
    place,
    field,
    east_c,
    north_c,
    mixing,
    linear,
    encode,
    west_in,
    east_in,
    south_in,
    north_in,
    *refs,
):
    coefs, diffused = refs[-2:]
    n_species, n_cols = west_in.shape
    n_reactions = encode.shape[1]
    cells = n_levels * n_rows
    lanes = lane_ids((1, n_cols))
    row_ids = lax.broadcasted_iota(jnp.int32, (n_rows, n_cols), 0)
    is_first, is_last = place[0] > 0, place[1] > 0
    CENTRE, EAST, WEST, NORTH, SOUTH, SCALE, LOWER, UPPER = range(8)

    upper = None
    for level in range(n_levels):
        ce, cn = east_c[level], north_c[level]
        east, west = jnp.maximum(ce, 0.0), jnp.minimum(ce, 0.0)
        north = jnp.where((row_ids == n_rows - 1) & is_last, 0.0, jnp.maximum(cn, 0.0))
        south = jnp.where((row_ids == 0) & is_first, 0.0, jnp.minimum(cn, 0.0))
        coefs[CENTRE, level] = 1.0 - east + west - north + south
        coefs[EAST, level] = east
        coefs[WEST, level] = west
        coefs[NORTH, level] = north
        coefs[SOUTH, level] = south
        pivot = 1.0
        if level > 0:
            below = mixing[level - 1]
            pivot = pivot + below - below * upper
        if level < n_levels - 1:
            pivot = pivot + mixing[level]
        scale = 1.0 / pivot
        coefs[SCALE, level] = scale
        if level > 0:
            coefs[LOWER, level] = below * scale
        if level < n_levels - 1:
            upper = mixing[level] * scale
            coefs[UPPER, level] = upper

    lit = jnp.zeros((1, n_cols), jnp.int32)
    for block in range(n_cols // BLOCK):
        lit = jnp.where(lanes // BLOCK == block, sun[0, block], lit)
    lit = lit > 0

    def coef(kind, level, r):
        return coefs[kind, level, pl.ds(r, 1), :]

    def transported(r):
        before, after = jnp.maximum(r - 1, 0), jnp.minimum(r + 1, n_rows - 1)
        swept = []
        for level in range(n_levels):
            at = level * n_rows + r
            value = field[level, r]
            from_west = jnp.where(
                lanes == 0,
                pltpu.roll(west_in[...], (n_cols + 1 - at) % n_cols, 1),
                pltpu.roll(value * coef(EAST, level, r), 1, 1),
            )
            from_east = jnp.where(
                lanes == n_cols - 1,
                pltpu.roll(east_in[...], n_cols - 1 - at, 1),
                pltpu.roll(value * coef(WEST, level, r), n_cols - 1, 1),
            )
            from_south = jnp.where(
                r == 0,
                south_in[level].astype(F32),
                field[level, before] * coef(NORTH, level, before),
            )
            from_north = jnp.where(
                r == n_rows - 1,
                north_in[level].astype(F32),
                field[level, after] * coef(SOUTH, level, after),
            )
            moved = value * coef(CENTRE, level, r) + (from_west - from_east) + (from_south - from_north)
            right = moved * coef(SCALE, level, r)
            if level > 0:
                right = right + coef(LOWER, level, r) * swept[-1]
            swept.append(right)
        for level in range(n_levels - 2, -1, -1):
            swept[level] = swept[level] + coef(UPPER, level, r) * swept[level + 1]
        return swept

    def product_of(rounded):
        both = jnp.dot(linear[...], rounded, preferred_element_type=F32)
        parts = [
            both[at : at + GROUP] * both[at + GROUP : at + 2 * GROUP]
            for at in range(0, 2 * n_reactions, 2 * GROUP)
        ]
        return jnp.concatenate(parts, axis=0).astype(BF16)

    def increments(tiles):
        rounded = [tile.astype(BF16) for tile in tiles]
        current = [value.astype(F32) for value in rounded]
        summed = [None] * len(tiles)
        units = [(substep, tile) for substep in range(SUBSTEPS) for tile in range(len(tiles))]
        rates = {}
        for at in range(len(units) + 1):
            if at < len(units):
                rates[at] = product_of(rounded[units[at][1]])
            if at > 0:
                substep, tile = units[at - 1]
                change = jnp.dot(encode[...], rates.pop(at - 1), preferred_element_type=F32)
                if substep == 0:
                    summed[tile] = change
                else:
                    summed[tile] = summed[tile] + change
                if substep < SUBSTEPS - 1:
                    current[tile] = current[tile] + change
                    rounded[tile] = current[tile].astype(BF16)
        return summed

    def transport_row(r, carry):
        for level, value in enumerate(transported(r)):
            diffused[level, r] = value
        return carry

    lax.fori_loop(0, n_rows, transport_row, 0)
    lit_pair = jnp.concatenate([lit, lit], axis=1)

    def rows(group, sides):
        places = [
            (level, group * ROWS_AT_ONCE + extra)
            for extra in range(ROWS_AT_ONCE)
            for level in range(0, n_levels, 2)
        ]
        tiles = [
            jnp.concatenate([diffused[level, r], diffused[level + 1, r]], axis=1)
            for level, r in places
        ]
        for (level, r), tile, change in zip(places, tiles, increments(tiles)):
            tile = tile + jnp.where(lit_pair, change, 0.0)
            for half in range(2):
                value = tile[:, half * n_cols : (half + 1) * n_cols]
                at = (level + half) * n_rows + r
                if last:
                    refs[0][pl.ds(at, n_species, stride=cells), :] = value
                else:
                    refs[0][level + half, r] = value
                    speed = east_c[level + half, pl.ds(r, 1), :]
                    side = jnp.where(
                        lanes == 0, jnp.minimum(speed, 0.0), jnp.maximum(speed, 0.0)
                    )
                    sides = pack_sides(value, side, at, *sides)
        return sides

    n_groups = n_rows // ROWS_AT_ONCE
    if last:
        lax.fori_loop(0, n_groups, rows, 0)
        return
    out, west, east, south, north = refs[:5]
    zeros = jnp.zeros((n_species, n_cols), F32)
    west[...], east[...] = lax.fori_loop(0, n_groups, rows, (zeros, zeros))
    for level in range(n_levels):
        for edge, send, clip in ((0, south, jnp.minimum), (n_rows - 1, north, jnp.maximum)):
            speed = clip(north_c[level, edge : edge + 1, :], 0.0)
            send[level] = (out[level, edge] * speed).astype(BF16)


def vmem(count):
    return [pl.BlockSpec(memory_space=pltpu.VMEM)] * count


def exchanged(west, east, south, north):
    lon, lat = lax.axis_size("lon"), lax.axis_size("lat")
    up = [(i, (i + 1) % lon) for i in range(lon)]
    down = [(j, i) for i, j in up]
    climb = [(i, i + 1) for i in range(lat - 1)]
    descend = [(j, i) for i, j in climb]
    from_south = lax.ppermute(north, "lat", climb)
    from_north = lax.ppermute(south, "lat", descend)
    from_west = lax.ppermute(east, "lon", up)
    from_east = lax.ppermute(west, "lon", down)
    return from_west, from_east, from_south, from_north


def on_device(
    latent_field,
    east_courant,
    north_courant,
    mixing,
    sunlit,
    decode_w,
    react_a,
    react_b,
    stoich,
    encode_w,
    rate_const,
):
    n_species, n_levels, n_rows, n_cols = latent_field.shape
    flat = (n_species * n_levels * n_rows, n_cols)
    layered = jax.ShapeDtypeStruct((n_levels, n_rows, n_species, n_cols), F32)
    side = jax.ShapeDtypeStruct((n_species, n_cols), F32)
    edge = jax.ShapeDtypeStruct((n_levels, n_species, n_cols), BF16)
    params = pltpu.CompilerParams(vmem_limit_bytes=VMEM_BYTES)
    field, *edges = pl.pallas_call(
        functools.partial(edge_kernel, n_levels, n_rows),
        out_shape=(layered, side, side, edge, edge),
        in_specs=vmem(3),
        out_specs=tuple(vmem(5)),
        compiler_params=params,
        name="edges",
    )(latent_field.reshape(flat), east_courant, north_courant)
    linear, encode = fold_weights(decode_w, react_a, react_b, stoich, encode_w, rate_const)
    lat_index = lax.axis_index("lat")
    place = jnp.stack([lat_index == 0, lat_index == lax.axis_size("lat") - 1]).astype(jnp.int32)
    for step in range(STEPS):
        last = step == STEPS - 1
        halos = exchanged(*edges)
        outs = pl.pallas_call(
            functools.partial(step_kernel, n_levels, n_rows, last),
            out_shape=(jax.ShapeDtypeStruct(flat, F32),)
            if last
            else (layered, side, side, edge, edge),
            in_specs=[pl.BlockSpec(memory_space=pltpu.SMEM)] * 2 + vmem(10),
            out_specs=tuple(vmem(1 if last else 5)),
            scratch_shapes=[
                pltpu.VMEM((8, n_levels, n_rows, n_cols), F32),
                pltpu.VMEM(layered.shape, F32),
            ],
            compiler_params=params,
            name="splitting_step",
        )(sunlit, place, field, east_courant, north_courant, mixing, linear, encode, *halos)
        field, edges = outs[0], outs[1:]
    return field.reshape(latent_field.shape)


def solution(mesh):
    placed = (
        P(None, None, "lat", "lon"),
        P(None, "lat", "lon"),
        P(None, "lat", "lon"),
        P(None, "lat", "lon"),
        P("lat", "lon"),
        P(),
        P(),
        P(),
        P(),
        P(),
        P(),
    )
    return jax.shard_map(
        on_device,
        mesh=mesh,
        in_specs=placed,
        out_specs=P(None, None, "lat", "lon"),
        check_vma=False,
    )
```

profile of v0, /device:TPU:0, one launch (start us, length us, event | category | flops | bytes accessed | tf_op | source)
XLA Modules:
  0.0 79.8 jit_solution(3024865091902063439)
XLA Ops:
  0.0 0.0 copy-start.8
  0.0 0.0 copy-start
  0.0 1.6 %copy-done = f32[32,8,16,128]{3,2,1,0:T(8,128)S(1)} copy-done((f32[32,8,16,128]{3,2,1,0:T(8,128)S(1)}, f32[32,8,16,128]{3,2,1,0:T(8,128)}, u32[]{:S(2)}) %copy-start) | copy-done | bytes 2097176
  1.6 0.0 copy-start.1
  1.6 0.8 %copy-done.1 = f32[8,16,128]{2,1,0:T(8,128)S(1)} copy-done((f32[8,16,128]{2,1,0:T(8,128)S(1)}, f32[8,16,128]{2,1,0:T(8,128)}, u32[]{:S(2)}) %copy-start.1) | copy-done | bytes 65560
  2.4 0.0 copy-start.3
  2.5 0.8 %copy-done.3 = f32[8,16,128]{2,1,0:T(8,128)S(1)} copy-done((f32[8,16,128]{2,1,0:T(8,128)S(1)}, f32[8,16,128]{2,1,0:T(8,128)}, u32[]{:S(2)}) %copy-start.3) | copy-done | bytes 65560
  3.3 0.0 copy-start.2
  3.3 0.0 copy-start.4
  3.3 0.0 copy-start.6
  3.3 2.5 %edges.1 = (f32[8,16,32,128]{3,2,1,0:T(8,128)S(1)}, f32[32,128]{1,0:T(8,128)S(1)}, f32[32,128]{1,0:T(8,128)S(1)}, bf16[8,32,128]{2,1,0:T(8,128)(2,1)S(1)}, bf16[8,32,128]{2,1,0:T(8,128)(2,1)S(1)}) custom-call(f32[4096,128]{1,0:T(8,128)S(1)} %bitcast.8, f32[8,16,128]{2,1,0:T(8,128)S(1)} %copy-done.1, f32[8,16,128]{2,1,0:T(8,128)S(1)} %copy-done.3), custom_call_target="tpu_custom_call" | custom-call | tf_op jit(solution)/shard_map/edges/pallas_call | solution.py:293
  5.8 3.0 %collective-permute-start = (f32[32,128]{1,0:T(8,128)S(1)}, f32[32,128]{1,0:T(8,128)S(1)}, u32[]{:S(2)}, u32[]{:S(2)}) collective-permute-start(f32[32,128]{1,0:T(8,128)S(1)} %get-tuple-element.20), channel_id=1, source_target_pairs={{0,1},{1,2},{2,3},{3,4},{4,5},{5,6},{6,7},{7,0},{8,9},{9,10},{10,1... | collective-permute-start | bytes 49160 | tf_op jit(solution)/shard_map/ppermute | solution.py:269
  8.8 3.1 %collective-permute-start.1 = (f32[32,128]{1,0:T(8,128)S(1)}, f32[32,128]{1,0:T(8,128)S(1)}, u32[]{:S(2)}, u32[]{:S(2)}) collective-permute-start(f32[32,128]{1,0:T(8,128)S(1)} %get-tuple-element.21), channel_id=1, source_target_pairs={{1,0},{2,1},{3,2},{4,3},{5,4},{6,5},{7,6},{0,7},{9,8},{10,9},{11,1... | collective-permute-start | bytes 49160 | tf_op jit(solution)/shard_map/ppermute | solution.py:270
  11.9 1.4 %collective-permute-start.2 = (bf16[8,32,128]{2,1,0:T(8,128)(2,1)S(1)}, bf16[8,32,128]{2,1,0:T(8,128)(2,1)S(1)}, u32[]{:S(2)}, u32[]{:S(2)}) collective-permute-start(bf16[8,32,128]{2,1,0:T(8,128)(2,1)S(1)} %get-tuple-element.22), channel_id=1, source_target_pairs={{0,8},{8,16},{16,24},{1,9},{9,17},{17,25},{2,10},{10,18},{18,26},{... | collective-permute-start | bytes 196616 | tf_op jit(solution)/shard_map/ppermute | solution.py:267
  13.3 1.3 %collective-permute-start.3 = (bf16[8,32,128]{2,1,0:T(8,128)(2,1)S(1)}, bf16[8,32,128]{2,1,0:T(8,128)(2,1)S(1)}, u32[]{:S(2)}, u32[]{:S(2)}) collective-permute-start(bf16[8,32,128]{2,1,0:T(8,128)(2,1)S(1)} %get-tuple-element.23), channel_id=1, source_target_pairs={{8,0},{16,8},{24,16},{9,1},{17,9},{25,17},{10,2},{18,10},{26,18},{... | collective-permute-start | bytes 196616 | tf_op jit(solution)/shard_map/ppermute | solution.py:268
  14.6 0.1 add_convert_fusion.place
  14.7 2.0 %fold_weights.1 = (bf16[512,32]{1,0:T(8,128)(2,1)}, bf16[32,256]{1,0:T(8,128)(2,1)}) custom-call(bf16[32,224]{1,0:T(8,128)(2,1)} %bitcast.11, bf16[224,256]{1,0:T(8,128)(2,1)} %bitcast.9, bf16[224,256]{1,0:T(8,128)(2,1)} %bitcast.10, bf16[224,256]{1,0:T(8,128)(2,1)} %stoich.1, bf16[32,224]{1,0:T(8,128)(2,1)} %encode.1, f32[1,256]{1,0:T(1,128)} %bitcast.12), custom_call_target="tpu_custom_call" | custom-call | flops 20000000 | bytes 500000 | tf_op jit(solution)/shard_map/fold_weights/pallas_call | solution.py:43
  16.7 0.0 collective-permute-done.west_in
  16.7 0.0 collective-permute-done.1.east_in
  16.7 0.0 collective-permute-done.2.south_in
  16.7 1.4 %collective-permute-done.3.north_in = bf16[8,32,128]{2,1,0:T(8,128)(2,1)S(1)} collective-permute-done((bf16[8,32,128]{2,1,0:T(8,128)(2,1)S(1)}, bf16[8,32,128]{2,1,0:T(8,128)(2,1)S(1)}, u32[]{:S(2)}, u32[]{:S(2)}) %collective-permute-start.3) | collective-permute-done | bytes 65568 | tf_op jit(solution)/shard_map/ppermute | solution.py:268
  18.1 0.0 copy-done.8
  18.1 0.0 copy-done.2
  18.1 0.0 copy-done.4
  18.2 0.0 copy-done.6
  18.2 0.0 copy-start.5
  18.2 0.9 %copy-done.5 = bf16[512,32]{1,0:T(8,128)(2,1)S(1)} copy-done((bf16[512,32]{1,0:T(8,128)(2,1)S(1)}, bf16[512,32]{1,0:T(8,128)(2,1)}, u32[]{:S(2)}) %copy-start.5) | copy-done | bytes 32792
  19.1 0.0 copy-start.7
  19.1 0.7 copy-done.7
  19.8 23.1 %splitting_step.2 = (f32[8,16,32,128]{3,2,1,0:T(8,128)S(1)}, f32[32,128]{1,0:T(8,128)S(1)}, f32[32,128]{1,0:T(8,128)S(1)}, bf16[8,32,128]{2,1,0:T(8,128)(2,1)S(1)}, bf16[8,32,128]{2,1,0:T(8,128)(2,1)S(1)}) custom-call(s32[1,8]{1,0:T(1,128)S(1)} %copy-done.8, s32[2]{0:T(128)S(1)} %add_convert_fusion.place, f32[8,16,32,128]{3,2,1,0:T(8,128)S(1)} %get-tuple-element.17.field, ...), custom_call_target="tpu_custom_call" | custom-call | tf_op jit(solution)/shard_map/splitting_step/pallas_call | solution.py:307
  42.9 4.8 %collective-permute-start.6 = (bf16[8,32,128]{2,1,0:T(8,128)(2,1)S(1)}, bf16[8,32,128]{2,1,0:T(8,128)(2,1)S(1)}, u32[]{:S(2)}, u32[]{:S(2)}) collective-permute-start(bf16[8,32,128]{2,1,0:T(8,128)(2,1)S(1)} %get-tuple-element.27), channel_id=1, source_target_pairs={{0,8},{8,16},{16,24},{1,9},{9,17},{17,25},{2,10},{10,18},{18,26},{... | collective-permute-start | bytes 196616 | tf_op jit(solution)/shard_map/ppermute | solution.py:267
  47.8 1.3 %collective-permute-start.7 = (bf16[8,32,128]{2,1,0:T(8,128)(2,1)S(1)}, bf16[8,32,128]{2,1,0:T(8,128)(2,1)S(1)}, u32[]{:S(2)}, u32[]{:S(2)}) collective-permute-start(bf16[8,32,128]{2,1,0:T(8,128)(2,1)S(1)} %get-tuple-element.28), channel_id=1, source_target_pairs={{8,0},{16,8},{24,16},{9,1},{17,9},{25,17},{10,2},{18,10},{26,18},{... | collective-permute-start | bytes 196616 | tf_op jit(solution)/shard_map/ppermute | solution.py:268
  49.1 0.1 collective-permute-start.4
  49.2 4.7 %collective-permute-start.5 = (f32[32,128]{1,0:T(8,128)S(1)}, f32[32,128]{1,0:T(8,128)S(1)}, u32[]{:S(2)}, u32[]{:S(2)}) collective-permute-start(f32[32,128]{1,0:T(8,128)S(1)} %get-tuple-element.26), channel_id=1, source_target_pairs={{1,0},{2,1},{3,2},{4,3},{5,4},{6,5},{7,6},{0,7},{9,8},{10,9},{11,1... | collective-permute-start | bytes 49160 | tf_op jit(solution)/shard_map/ppermute | solution.py:270
  53.9 1.7 %collective-permute-done.4.west_in = f32[32,128]{1,0:T(8,128)S(1)} collective-permute-done((f32[32,128]{1,0:T(8,128)S(1)}, f32[32,128]{1,0:T(8,128)S(1)}, u32[]{:S(2)}, u32[]{:S(2)}) %collective-permute-start.4) | collective-permute-done | bytes 16416 | tf_op jit(solution)/shard_map/ppermute | solution.py:269
  55.6 0.0 collective-permute-done.5.east_in
  55.6 0.0 collective-permute-done.6.south_in
  55.6 0.0 collective-permute-done.7.north_in
  55.6 24.2 %splitting_step.3 = f32[4096,128]{1,0:T(8,128)} custom-call(s32[1,8]{1,0:T(1,128)S(1)} %copy-done.8, s32[2]{0:T(128)S(1)} %add_convert_fusion.place, f32[8,16,32,128]{3,2,1,0:T(8,128)S(1)} %get-tuple-element.24.field, f32[8,16,128]{2,1,0:T(8,128)S(1)} %copy-done.2, f32[8,16,128]{2,1,0:T(8,128)S(1)} %copy-done.4, f32[7,16,128]{2,1,0:T(8,128)S(1)} %copy-done.6, ...), custom_call_target="tpu_custom_call" | custom-call | tf_op jit(solution)/shard_map/splitting_step/pallas_call | solution.py:307
Async XLA Ops:
  0.0 18.1 %copy-start.8 = (s32[1,8]{1,0:T(1,128)S(1)}, s32[1,8]{1,0:T(1,128)}, u32[]{:S(2)}) copy-start(s32[1,8]{1,0:T(1,128)} %sun.3) | copy-start | bytes 100
  0.0 1.6 %copy-start = (f32[32,8,16,128]{3,2,1,0:T(8,128)S(1)}, f32[32,8,16,128]{3,2,1,0:T(8,128)}, u32[]{:S(2)}) copy-start(f32[32,8,16,128]{3,2,1,0:T(8,128)} %param.11) | copy-start | bytes 6291460
  1.6 0.8 %copy-start.1 = (f32[8,16,128]{2,1,0:T(8,128)S(1)}, f32[8,16,128]{2,1,0:T(8,128)}, u32[]{:S(2)}) copy-start(f32[8,16,128]{2,1,0:T(8,128)} %east_c.5) | copy-start | bytes 196612
  2.4 0.8 %copy-start.3 = (f32[8,16,128]{2,1,0:T(8,128)S(1)}, f32[8,16,128]{2,1,0:T(8,128)}, u32[]{:S(2)}) copy-start(f32[8,16,128]{2,1,0:T(8,128)} %north_c.5) | copy-start | bytes 196612
  3.3 14.9 %copy-start.2 = (f32[8,16,128]{2,1,0:T(8,128)S(1)}, f32[8,16,128]{2,1,0:T(8,128)}, u32[]{:S(2)}) copy-start(f32[8,16,128]{2,1,0:T(8,128)} %east_c.5) | copy-start | bytes 196612
  3.3 14.9 %copy-start.4 = (f32[8,16,128]{2,1,0:T(8,128)S(1)}, f32[8,16,128]{2,1,0:T(8,128)}, u32[]{:S(2)}) copy-start(f32[8,16,128]{2,1,0:T(8,128)} %north_c.5) | copy-start | bytes 196612
  3.3 14.9 %copy-start.6 = (f32[7,16,128]{2,1,0:T(8,128)S(1)}, f32[7,16,128]{2,1,0:T(8,128)}, u32[]{:S(2)}) copy-start(f32[7,16,128]{2,1,0:T(8,128)} %mixing.3) | copy-start | bytes 172036
  5.8 10.9 %collective-permute-start = (f32[32,128]{1,0:T(8,128)S(1)}, f32[32,128]{1,0:T(8,128)S(1)}, u32[]{:S(2)}, u32[]{:S(2)}) collective-permute-start(f32[32,128]{1,0:T(8,128)S(1)} %get-tuple-element.20), channel_id=1, source_target_pairs={{0,1},{1,2},{2,3},{3,4},{4,5},{5,6},{6,7},{7,0},{8,9},{9,10},{10,1... | collective-permute-start | bytes 49160 | tf_op jit(solution)/shard_map/ppermute | solution.py:269
  8.8 7.9 %collective-permute-start.1 = (f32[32,128]{1,0:T(8,128)S(1)}, f32[32,128]{1,0:T(8,128)S(1)}, u32[]{:S(2)}, u32[]{:S(2)}) collective-permute-start(f32[32,128]{1,0:T(8,128)S(1)} %get-tuple-element.21), channel_id=1, source_target_pairs={{1,0},{2,1},{3,2},{4,3},{5,4},{6,5},{7,6},{0,7},{9,8},{10,9},{11,1... | collective-permute-start | bytes 49160 | tf_op jit(solution)/shard_map/ppermute | solution.py:270
  11.9 4.8 %collective-permute-start.2 = (bf16[8,32,128]{2,1,0:T(8,128)(2,1)S(1)}, bf16[8,32,128]{2,1,0:T(8,128)(2,1)S(1)}, u32[]{:S(2)}, u32[]{:S(2)}) collective-permute-start(bf16[8,32,128]{2,1,0:T(8,128)(2,1)S(1)} %get-tuple-element.22), channel_id=1, source_target_pairs={{0,8},{8,16},{16,24},{1,9},{9,17},{17,25},{2,10},{10,18},{18,26},{... | collective-permute-start | bytes 196616 | tf_op jit(solution)/shard_map/ppermute | solution.py:267
  13.3 4.8 %collective-permute-start.3 = (bf16[8,32,128]{2,1,0:T(8,128)(2,1)S(1)}, bf16[8,32,128]{2,1,0:T(8,128)(2,1)S(1)}, u32[]{:S(2)}, u32[]{:S(2)}) collective-permute-start(bf16[8,32,128]{2,1,0:T(8,128)(2,1)S(1)} %get-tuple-element.23), channel_id=1, source_target_pairs={{8,0},{16,8},{24,16},{9,1},{17,9},{25,17},{10,2},{18,10},{26,18},{... | collective-permute-start | bytes 196616 | tf_op jit(solution)/shard_map/ppermute | solution.py:268
  18.2 0.9 %copy-start.5 = (bf16[512,32]{1,0:T(8,128)(2,1)S(1)}, bf16[512,32]{1,0:T(8,128)(2,1)}, u32[]{:S(2)}) copy-start(bf16[512,32]{1,0:T(8,128)(2,1)} %get-tuple-element.18.linear) | copy-start | bytes 98308
  19.1 0.7 copy-start.7
  42.9 12.7 %collective-permute-start.6 = (bf16[8,32,128]{2,1,0:T(8,128)(2,1)S(1)}, bf16[8,32,128]{2,1,0:T(8,128)(2,1)S(1)}, u32[]{:S(2)}, u32[]{:S(2)}) collective-permute-start(bf16[8,32,128]{2,1,0:T(8,128)(2,1)S(1)} %get-tuple-element.27), channel_id=1, source_target_pairs={{0,8},{8,16},{16,24},{1,9},{9,17},{17,25},{2,10},{10,18},{18,26},{... | collective-permute-start | bytes 196616 | tf_op jit(solution)/shard_map/ppermute | solution.py:267
  47.8 7.8 %collective-permute-start.7 = (bf16[8,32,128]{2,1,0:T(8,128)(2,1)S(1)}, bf16[8,32,128]{2,1,0:T(8,128)(2,1)S(1)}, u32[]{:S(2)}, u32[]{:S(2)}) collective-permute-start(bf16[8,32,128]{2,1,0:T(8,128)(2,1)S(1)} %get-tuple-element.28), channel_id=1, source_target_pairs={{8,0},{16,8},{24,16},{9,1},{17,9},{25,17},{10,2},{18,10},{26,18},{... | collective-permute-start | bytes 196616 | tf_op jit(solution)/shard_map/ppermute | solution.py:268
  49.1 6.5 %collective-permute-start.4 = (f32[32,128]{1,0:T(8,128)S(1)}, f32[32,128]{1,0:T(8,128)S(1)}, u32[]{:S(2)}, u32[]{:S(2)}) collective-permute-start(f32[32,128]{1,0:T(8,128)S(1)} %get-tuple-element.25), channel_id=1, source_target_pairs={{0,1},{1,2},{2,3},{3,4},{4,5},{5,6},{6,7},{7,0},{8,9},{9,10},{10,1... | collective-permute-start | bytes 49160 | tf_op jit(solution)/shard_map/ppermute | solution.py:269
  49.2 6.4 %collective-permute-start.5 = (f32[32,128]{1,0:T(8,128)S(1)}, f32[32,128]{1,0:T(8,128)S(1)}, u32[]{:S(2)}, u32[]{:S(2)}) collective-permute-start(f32[32,128]{1,0:T(8,128)S(1)} %get-tuple-element.26), channel_id=1, source_target_pairs={{1,0},{2,1},{3,2},{4,3},{5,4},{6,5},{7,6},{0,7},{9,8},{10,9},{11,1... | collective-permute-start | bytes 49160 | tf_op jit(solution)/shard_map/ppermute | solution.py:270
where the time goes:
time: 80.2 us; the launch traced here: 79.8 us
  Pallas kernels  51.8 us (65%)
  starting transfers between devices  19.8 us (25%)
  local copies, waits for them, and re-layouts  4.91 us (6%)
  waiting for transfers between devices  3.18 us (4%)
    pallas_call x2, Pallas kernels, on_device(): pl.pallas_call(functools.partial(step_kernel, n_levels, n_rows, last), ou...  47.4 us
    ppermute x2, starting transfers between devices, exchanged(): from_east = lax.ppermute(west, 'lon', down)  7.81 us
    ppermute x2, starting transfers between devices, exchanged(): from_south = lax.ppermute(north, 'lat', climb)  6.29 us
    unnamed x18, local copies, waits for them, and re-layouts  4.91 us
    ppermute x2, starting transfers between devices, exchanged(): from_west = lax.ppermute(east, 'lon', up)  3.08 us
    ppermute x2, starting transfers between devices, exchanged(): from_north = lax.ppermute(south, 'lat', descend)  2.58 us
    pallas_call x1, Pallas kernels, on_device(): pl.pallas_call(functools.partial(edge_kernel, n_levels, n_rows), out_shap...  2.46 us
    pallas_call x1, Pallas kernels, fold_weights(): pl.pallas_call(fold_kernel, out_shape=(jax.ShapeDtypeStruct((2 * n_reacti...  1.96 us
  transfers between devices with their start and end apart: 8, of which 2 were waited for; matrix products, arithmetic and copies ran while one was open for 0% of the time, Pallas kernels for 2%

commit v1 on v0

--- a/solution.py
+++ b/solution.py
@@ -12,6 +12,7 @@
 STEPS = 2
 GROUP = 16
 ROWS_AT_ONCE = 2
+LEVELS_AT_ONCE = 8
 
 F32 = jnp.float32
 BF16 = jnp.bfloat16
@@ -46,6 +47,8 @@
             jax.ShapeDtypeStruct((2 * n_reactions, n_species), BF16),
             jax.ShapeDtypeStruct((n_species, n_reactions), BF16),
         ),
+        out_specs=tuple(vmem(2)),
+        compiler_params=pltpu.CompilerParams(vmem_limit_bytes=VMEM_BYTES),
         cost_estimate=pl.CostEstimate(flops=20_000_000, bytes_accessed=500_000, transcendentals=0),
         name="fold_weights",
     )(decode_w.T, react_a.T, react_b.T, stoich, encode_w, rate_const[None])
@@ -60,27 +63,38 @@
     return west, east
 
 
-def edge_kernel(n_levels, n_rows, latent, east_c, north_c, moved_out, west, east, south, north):
-    n_species, n_cols = west.shape
-    cells = n_levels * n_rows
+def edge_kernel(place, latent, east_c, north_c, moved_out, west, east, south, north, *scratch):
+    tiles, east_v, north_v, sems = scratch
+    n_levels, n_species, n_rows, n_cols = tiles.shape
     lanes = lane_ids((1, n_cols))
-
-    def row(r, sides):
-        for level in range(n_levels):
+    copies = [
+        pltpu.make_async_copy(east_c, east_v, sems.at[n_levels]),
+        pltpu.make_async_copy(north_c, north_v, sems.at[n_levels + 1]),
+    ]
+    for level in range(n_levels):
+        copies.append(
+            pltpu.make_async_copy(latent.at[:, level], tiles.at[level], sems.at[level])
+        )
+    for copy in copies:
+        copy.start()
+    copies[0].wait()
+    copies[1].wait()
+    sides = (jnp.zeros((n_species, n_cols), F32),) * 2
+    for level in range(n_levels):
+        copies[2 + level].wait()
+        tile = tiles.at[level].reshape(n_species * n_rows, n_cols)
+        for r in range(n_rows):
             at = level * n_rows + r
-            value = latent[pl.ds(at, n_species, stride=cells), :]
+            value = tile[pl.ds(r, n_species, stride=n_rows), :]
             moved_out[level, r] = value
-            speed = east_c[level, pl.ds(r, 1), :]
+            speed = east_v[level, r : r + 1, :]
             coef = jnp.where(lanes == 0, jnp.minimum(speed, 0.0), jnp.maximum(speed, 0.0))
             sides = pack_sides(value, coef, at, *sides)
-        return sides
-
-    zeros = jnp.zeros((n_species, n_cols), F32)
-    west[...], east[...] = lax.fori_loop(0, n_rows, row, (zeros, zeros))
-    for level in range(n_levels):
-        for edge, out, clip in ((0, south, jnp.minimum), (n_rows - 1, north, jnp.maximum)):
-            speed = clip(north_c[level, edge : edge + 1, :], 0.0)
-            out[level] = (moved_out[level, edge] * speed).astype(BF16)
+        low = jnp.minimum(north_v[level, :1, :], 0.0)
+        south[level] = (moved_out[level, 0] * jnp.where(place[0] > 0, 0.0, low)).astype(BF16)
+        high = jnp.maximum(north_v[level, n_rows - 1 :, :], 0.0)
+        north[level] = (moved_out[level, n_rows - 1] * jnp.where(place[1] > 0, 0.0, high)).astype(BF16)
+    west[...], east[...] = sides
 
 
 def step_kernel(
@@ -213,21 +227,23 @@
         return carry
 
     lax.fori_loop(0, n_rows, transport_row, 0)
-    lit_pair = jnp.concatenate([lit, lit], axis=1)
+    lit_tile = jnp.concatenate([lit] * LEVELS_AT_ONCE, axis=1)
 
     def rows(group, sides):
         places = [
             (level, group * ROWS_AT_ONCE + extra)
             for extra in range(ROWS_AT_ONCE)
-            for level in range(0, n_levels, 2)
+            for level in range(0, n_levels, LEVELS_AT_ONCE)
         ]
         tiles = [
-            jnp.concatenate([diffused[level, r], diffused[level + 1, r]], axis=1)
+            jnp.concatenate(
+                [diffused[level + extra, r] for extra in range(LEVELS_AT_ONCE)], axis=1
+            )
             for level, r in places
         ]
         for (level, r), tile, change in zip(places, tiles, increments(tiles)):
-            tile = tile + jnp.where(lit_pair, change, 0.0)
-            for half in range(2):
+            tile = tile + jnp.where(lit_tile, change, 0.0)
+            for half in range(LEVELS_AT_ONCE):
                 value = tile[:, half * n_cols : (half + 1) * n_cols]
                 at = (level + half) * n_rows + r
                 if last:
@@ -249,9 +265,8 @@
     zeros = jnp.zeros((n_species, n_cols), F32)
     west[...], east[...] = lax.fori_loop(0, n_groups, rows, (zeros, zeros))
     for level in range(n_levels):
-        for edge, send, clip in ((0, south, jnp.minimum), (n_rows - 1, north, jnp.maximum)):
-            speed = clip(north_c[level, edge : edge + 1, :], 0.0)
-            send[level] = (out[level, edge] * speed).astype(BF16)
+        for edge, send, kind in ((0, south, SOUTH), (n_rows - 1, north, NORTH)):
+            send[level] = (out[level, edge] * coefs[kind, level, edge : edge + 1]).astype(BF16)
 
 
 def vmem(count):
@@ -262,7 +277,7 @@
     lon, lat = lax.axis_size("lon"), lax.axis_size("lat")
     up = [(i, (i + 1) % lon) for i in range(lon)]
     down = [(j, i) for i, j in up]
-    climb = [(i, i + 1) for i in range(lat - 1)]
+    climb = [(i, (i + 1) % lat) for i in range(lat)]
     descend = [(j, i) for i, j in climb]
     from_south = lax.ppermute(north, "lat", climb)
     from_north = lax.ppermute(south, "lat", descend)
@@ -290,17 +305,25 @@
     side = jax.ShapeDtypeStruct((n_species, n_cols), F32)
     edge = jax.ShapeDtypeStruct((n_levels, n_species, n_cols), BF16)
     params = pltpu.CompilerParams(vmem_limit_bytes=VMEM_BYTES)
+    lat_index = lax.axis_index("lat")
+    place = jnp.stack([lat_index == 0, lat_index == lax.axis_size("lat") - 1]).astype(jnp.int32)
+    smem = pl.BlockSpec(memory_space=pltpu.SMEM)
+    hbm = pl.BlockSpec(memory_space=pltpu.HBM)
     field, *edges = pl.pallas_call(
-        functools.partial(edge_kernel, n_levels, n_rows),
+        edge_kernel,
         out_shape=(layered, side, side, edge, edge),
-        in_specs=vmem(3),
+        in_specs=[smem, hbm, hbm, hbm],
         out_specs=tuple(vmem(5)),
+        scratch_shapes=[
+            pltpu.VMEM((n_levels, n_species, n_rows, n_cols), F32),
+            pltpu.VMEM((n_levels, n_rows, n_cols), F32),
+            pltpu.VMEM((n_levels, n_rows, n_cols), F32),
+            pltpu.SemaphoreType.DMA((n_levels + 2,)),
+        ],
         compiler_params=params,
         name="edges",
-    )(latent_field.reshape(flat), east_courant, north_courant)
+    )(place, latent_field, east_courant, north_courant)
     linear, encode = fold_weights(decode_w, react_a, react_b, stoich, encode_w, rate_const)
-    lat_index = lax.axis_index("lat")
-    place = jnp.stack([lat_index == 0, lat_index == lax.axis_size("lat") - 1]).astype(jnp.int32)
     for step in range(STEPS):
         last = step == STEPS - 1
         halos = exchanged(*edges)
@@ -309,7 +332,7 @@
             out_shape=(jax.ShapeDtypeStruct(flat, F32),)
             if last
             else (layered, side, side, edge, edge),
-            in_specs=[pl.BlockSpec(memory_space=pltpu.SMEM)] * 2 + vmem(10),
+            in_specs=[smem] * 2 + vmem(10),
             out_specs=tuple(vmem(1 if last else 5)),
             scratch_shapes=[
                 pltpu.VMEM((8, n_levels, n_rows, n_cols), F32),

time: 80.2 us -> 61.6 us (0.77)
  Pallas kernels: 51.8 us -> 40.4 us
  starting transfers between devices: 19.8 us -> 14.3 us
  local copies, waits for them, and re-layouts: 4.91 us -> 3.31 us
    pallas_call x2, Pallas kernels: 47.4 us -> 37.9 us  [on_device(): pl.pallas_call(functools.partial(step_kernel, n_levels, n_rows, last), ou...]
    ppermute x2, starting transfers between devices: 6.29 us -> 0.56 us  [exchanged(): from_south = lax.ppermute(north, 'lat', climb)]
    pallas_call x1, Pallas kernels: 1.96 us -> 0.28 us  [fold_weights(): pl.pallas_call(fold_kernel, out_shape=(jax.ShapeDtypeStruct((2 * n_reacti...]
    unnamed x18 -> x24, local copies, waits for them, and re-layouts: 4.91 us -> 3.31 us
    ppermute x2, starting transfers between devices: 7.81 us -> 6.37 us  [exchanged(): from_east = lax.ppermute(west, 'lon', down)]
    ppermute x2, waiting for transfers between devices: 1.44 us -> 0.01 us  [exchanged(): from_north = lax.ppermute(south, 'lat', descend)]
    ppermute x2, waiting for transfers between devices: 1.73 us -> 3.1 us  [exchanged(): from_west = lax.ppermute(east, 'lon', up)]
    ppermute x2, starting transfers between devices: 2.58 us -> 3.72 us  [exchanged(): from_north = lax.ppermute(south, 'lat', descend)]
  transfers between devices with their start and end apart: 8 -> 8, of which waited for: 2 -> 2; matrix products, arithmetic and copies ran while one was open for 0% -> 0% of each run, Pallas kernels for 2% -> 0%
where the time goes in v1:
time: 61.6 us; the launch traced here: 61.3 us
  Pallas kernels  40.4 us (66%)
  starting transfers between devices  14.3 us (23%)
  local copies, waits for them, and re-layouts  3.31 us (5%)
  waiting for transfers between devices  3.12 us (5%)
    pallas_call x2, Pallas kernels, on_device(): pl.pallas_call(functools.partial(step_kernel, n_levels, n_rows, last), ou...  37.9 us
    ppermute x2, starting transfers between devices, exchanged(): from_east = lax.ppermute(west, 'lon', down)  6.37 us
    ppermute x2, starting transfers between devices, exchanged(): from_north = lax.ppermute(south, 'lat', descend)  3.72 us
    ppermute x2, starting transfers between devices, exchanged(): from_west = lax.ppermute(east, 'lon', up)  3.66 us
    unnamed x24, local copies, waits for them, and re-layouts  3.31 us
    ppermute x2, waiting for transfers between devices, exchanged(): from_west = lax.ppermute(east, 'lon', up)  3.1 us
    pallas_call x1, Pallas kernels, on_device(): pl.pallas_call(edge_kernel, out_shape=(layered, side, side, edge, edge),...  2.25 us
  transfers between devices with their start and end apart: 8, of which 2 were waited for; matrix products, arithmetic and copies ran while one was open for 0% of the time, Pallas kernels for 0%

profile of v1, /device:TPU:0, one launch (start us, length us, event | category | flops | bytes accessed | tf_op | source)
XLA Modules:
  0.0 61.3 jit_solution(10546702935597644740)
XLA Ops:
  0.0 0.0 copy-start.8
  0.0 0.0 copy-start.10
  0.0 0.1 add_convert_fusion.place
  0.1 0.0 copy-start
  0.1 1.6 %copy-done = f32[32,8,16,128]{3,2,1,0:T(8,128)S(1)} copy-done((f32[32,8,16,128]{3,2,1,0:T(8,128)S(1)}, f32[32,8,16,128]{3,2,1,0:T(8,128)}, u32[]{:S(2)}) %copy-start) | copy-done | bytes 2097176
  1.7 0.0 copy-start.1
  1.7 0.8 %copy-done.1 = f32[8,16,128]{2,1,0:T(8,128)S(1)} copy-done((f32[8,16,128]{2,1,0:T(8,128)S(1)}, f32[8,16,128]{2,1,0:T(8,128)}, u32[]{:S(2)}) %copy-start.1) | copy-done | bytes 65560
  2.5 0.0 copy-start.2
  2.5 0.8 %copy-done.2 = f32[8,16,128]{2,1,0:T(8,128)S(1)} copy-done((f32[8,16,128]{2,1,0:T(8,128)S(1)}, f32[8,16,128]{2,1,0:T(8,128)}, u32[]{:S(2)}) %copy-start.2) | copy-done | bytes 65560
  3.4 0.0 copy-start.5
  3.4 0.0 copy-start.6
  3.4 0.0 copy-start.7
  3.4 0.0 copy-start.9
  3.4 0.0 copy-start.11
  3.4 0.0 copy-start.3
  3.4 0.0 copy-start.4
  3.4 2.2 %edges.1 = (f32[8,16,32,128]{3,2,1,0:T(8,128)S(1)}, f32[32,128]{1,0:T(8,128)S(1)}, f32[32,128]{1,0:T(8,128)S(1)}, bf16[8,32,128]{2,1,0:T(8,128)(2,1)S(1)}, bf16[8,32,128]{2,1,0:T(8,128)(2,1)S(1)}) custom-call(s32[2]{0:T(128)S(1)} %add_convert_fusion.place, f32[32,8,16,128]{3,2,1,0:T(8,128)S(1)} %copy-done, f32[8,16,128]{2,1,0:T(8,128)S(1)} %copy-done.1, ...), custom_call_target="tpu_custom_call" | custom-call | tf_op jit(solution)/shard_map/edges/pallas_call | solution.py:312
  5.7 0.5 collective-permute-start.2
  6.2 2.0 %collective-permute-start.3 = (bf16[8,32,128]{2,1,0:T(8,128)(2,1)S(1)}, bf16[8,32,128]{2,1,0:T(8,128)(2,1)S(1)}, u32[]{:S(2)}, u32[]{:S(2)}) collective-permute-start(bf16[8,32,128]{2,1,0:T(8,128)(2,1)S(1)} %get-tuple-element.23), channel_id=1, source_target_pairs={{8,0},{16,8},{24,16},{0,24},{9,1},{17,9},{25,17},{1,25},{10,2},{18... | collective-permute-start | bytes 196616 | tf_op jit(solution)/shard_map/ppermute | solution.py:283
  8.1 2.3 %collective-permute-start = (f32[32,128]{1,0:T(8,128)S(1)}, f32[32,128]{1,0:T(8,128)S(1)}, u32[]{:S(2)}, u32[]{:S(2)}) collective-permute-start(f32[32,128]{1,0:T(8,128)S(1)} %get-tuple-element.20), channel_id=1, source_target_pairs={{0,1},{1,2},{2,3},{3,4},{4,5},{5,6},{6,7},{7,0},{8,9},{9,10},{10,1... | collective-permute-start | bytes 49160 | tf_op jit(solution)/shard_map/ppermute | solution.py:284
  10.4 3.0 %collective-permute-start.1 = (f32[32,128]{1,0:T(8,128)S(1)}, f32[32,128]{1,0:T(8,128)S(1)}, u32[]{:S(2)}, u32[]{:S(2)}) collective-permute-start(f32[32,128]{1,0:T(8,128)S(1)} %get-tuple-element.21), channel_id=1, source_target_pairs={{1,0},{2,1},{3,2},{4,3},{5,4},{6,5},{7,6},{0,7},{9,8},{10,9},{11,1... | collective-permute-start | bytes 49160 | tf_op jit(solution)/shard_map/ppermute | solution.py:285
  13.5 0.0 copy-done.8
  13.5 0.0 copy-done.5
  13.5 0.0 copy-done.6
  13.5 0.0 copy-done.7
  13.5 0.0 copy-done.9
  13.5 0.0 copy-done.11
  13.5 0.3 fold_weights.1
  13.8 1.4 %collective-permute-done.west_in = f32[32,128]{1,0:T(8,128)S(1)} collective-permute-done((f32[32,128]{1,0:T(8,128)S(1)}, f32[32,128]{1,0:T(8,128)S(1)}, u32[]{:S(2)}, u32[]{:S(2)}) %collective-permute-start) | collective-permute-done | bytes 16416 | tf_op jit(solution)/shard_map/ppermute | solution.py:284
  15.2 0.0 collective-permute-done.1.east_in
  15.2 0.0 collective-permute-done.2.south_in
  15.2 0.0 collective-permute-done.3.north_in
  15.2 0.0 copy-done.10
  15.2 0.0 copy-done.3
  15.2 0.0 copy-done.4
  15.2 18.1 %splitting_step.2 = (f32[8,16,32,128]{3,2,1,0:T(8,128)S(1)}, f32[32,128]{1,0:T(8,128)S(1)}, f32[32,128]{1,0:T(8,128)S(1)}, bf16[8,32,128]{2,1,0:T(8,128)(2,1)S(1)}, bf16[8,32,128]{2,1,0:T(8,128)(2,1)S(1)}) custom-call(s32[1,8]{1,0:T(1,128)S(1)} %copy-done.10, s32[2]{0:T(128)S(1)} %add_convert_fusion.place, f32[8,16,32,128]{3,2,1,0:T(8,128)S(1)} %get-tuple-element.17.field, ...), custom_call_target="tpu_custom_call" | custom-call | tf_op jit(solution)/shard_map/splitting_step/pallas_call | solution.py:330
  33.3 0.1 collective-permute-start.6
  33.4 1.7 %collective-permute-start.7 = (bf16[8,32,128]{2,1,0:T(8,128)(2,1)S(1)}, bf16[8,32,128]{2,1,0:T(8,128)(2,1)S(1)}, u32[]{:S(2)}, u32[]{:S(2)}) collective-permute-start(bf16[8,32,128]{2,1,0:T(8,128)(2,1)S(1)} %get-tuple-element.28), channel_id=1, source_target_pairs={{8,0},{16,8},{24,16},{0,24},{9,1},{17,9},{25,17},{1,25},{10,2},{18... | collective-permute-start | bytes 196616 | tf_op jit(solution)/shard_map/ppermute | solution.py:283
  35.1 1.4 %collective-permute-start.4 = (f32[32,128]{1,0:T(8,128)S(1)}, f32[32,128]{1,0:T(8,128)S(1)}, u32[]{:S(2)}, u32[]{:S(2)}) collective-permute-start(f32[32,128]{1,0:T(8,128)S(1)} %get-tuple-element.25), channel_id=1, source_target_pairs={{0,1},{1,2},{2,3},{3,4},{4,5},{5,6},{6,7},{7,0},{8,9},{9,10},{10,1... | collective-permute-start | bytes 49160 | tf_op jit(solution)/shard_map/ppermute | solution.py:284
  36.5 3.3 %collective-permute-start.5 = (f32[32,128]{1,0:T(8,128)S(1)}, f32[32,128]{1,0:T(8,128)S(1)}, u32[]{:S(2)}, u32[]{:S(2)}) collective-permute-start(f32[32,128]{1,0:T(8,128)S(1)} %get-tuple-element.26), channel_id=1, source_target_pairs={{1,0},{2,1},{3,2},{4,3},{5,4},{6,5},{7,6},{0,7},{9,8},{10,9},{11,1... | collective-permute-start | bytes 49160 | tf_op jit(solution)/shard_map/ppermute | solution.py:285
  39.8 1.7 %collective-permute-done.4.west_in = f32[32,128]{1,0:T(8,128)S(1)} collective-permute-done((f32[32,128]{1,0:T(8,128)S(1)}, f32[32,128]{1,0:T(8,128)S(1)}, u32[]{:S(2)}, u32[]{:S(2)}) %collective-permute-start.4) | collective-permute-done | bytes 16416 | tf_op jit(solution)/shard_map/ppermute | solution.py:284
  41.5 0.0 collective-permute-done.5.east_in
  41.5 0.0 collective-permute-done.6.south_in
  41.5 0.0 collective-permute-done.7.north_in
  41.5 19.8 %splitting_step.3 = f32[4096,128]{1,0:T(8,128)} custom-call(s32[1,8]{1,0:T(1,128)S(1)} %copy-done.10, s32[2]{0:T(128)S(1)} %add_convert_fusion.place, f32[8,16,32,128]{3,2,1,0:T(8,128)S(1)} %get-tuple-element.24.field, f32[8,16,128]{2,1,0:T(8,128)S(1)} %copy-done.1, f32[8,16,128]{2,1,0:T(8,128)S(1)} %copy-done.3, f32[7,16,128]{2,1,0:T(8,128)S(1)} %copy-done.4, ...), custom_call_target="tpu_custom_call" | custom-call | tf_op jit(solution)/shard_map/splitting_step/pallas_call | solution.py:330
Async XLA Ops:
  0.0 13.5 %copy-start.8 = (bf16[224,32]{0,1:T(8,128)(2,1)S(1)}, bf16[224,32]{0,1:T(8,128)(2,1)}, u32[]{:S(2)}) copy-start(bf16[224,32]{0,1:T(8,128)(2,1)} %param.16) | copy-start | bytes 43012
  0.0 15.2 %copy-start.10 = (s32[1,8]{1,0:T(1,128)S(1)}, s32[1,8]{1,0:T(1,128)}, u32[]{:S(2)}) copy-start(s32[1,8]{1,0:T(1,128)} %sun.3) | copy-start | bytes 100
  0.1 1.6 %copy-start = (f32[32,8,16,128]{3,2,1,0:T(8,128)S(1)}, f32[32,8,16,128]{3,2,1,0:T(8,128)}, u32[]{:S(2)}) copy-start(f32[32,8,16,128]{3,2,1,0:T(8,128)} %latent.1) | copy-start | bytes 6291460
  1.7 0.8 %copy-start.1 = (f32[8,16,128]{2,1,0:T(8,128)S(1)}, f32[8,16,128]{2,1,0:T(8,128)}, u32[]{:S(2)}) copy-start(f32[8,16,128]{2,1,0:T(8,128)} %east_c.5) | copy-start | bytes 196612
  2.5 0.8 %copy-start.2 = (f32[8,16,128]{2,1,0:T(8,128)S(1)}, f32[8,16,128]{2,1,0:T(8,128)}, u32[]{:S(2)}) copy-start(f32[8,16,128]{2,1,0:T(8,128)} %north_c.5) | copy-start | bytes 196612
  3.4 10.1 %copy-start.5 = (bf16[256,224]{0,1:T(8,128)(2,1)S(1)}, bf16[256,224]{0,1:T(8,128)(2,1)}, u32[]{:S(2)}) copy-start(bf16[256,224]{0,1:T(8,128)(2,1)} %param.17) | copy-start | bytes 344068
  3.4 10.1 %copy-start.6 = (bf16[256,224]{0,1:T(8,128)(2,1)S(1)}, bf16[256,224]{0,1:T(8,128)(2,1)}, u32[]{:S(2)}) copy-start(bf16[256,224]{0,1:T(8,128)(2,1)} %param.18) | copy-start | bytes 344068
  3.4 10.1 %copy-start.7 = (bf16[224,256]{1,0:T(8,128)(2,1)S(1)}, bf16[224,256]{1,0:T(8,128)(2,1)}, u32[]{:S(2)}) copy-start(bf16[224,256]{1,0:T(8,128)(2,1)} %stoich.1) | copy-start | bytes 344068
  3.4 10.1 %copy-start.9 = (bf16[32,224]{1,0:T(8,128)(2,1)S(1)}, bf16[32,224]{1,0:T(8,128)(2,1)}, u32[]{:S(2)}) copy-start(bf16[32,224]{1,0:T(8,128)(2,1)} %encode.1) | copy-start | bytes 43012
  3.4 10.1 %copy-start.11 = (f32[256]{0:T(256)S(1)}, f32[256]{0:T(256)}, u32[]{:S(2)}) copy-start(f32[256]{0:T(256)} %param.21) | copy-start | bytes 3076
  3.4 11.8 %copy-start.3 = (f32[8,16,128]{2,1,0:T(8,128)S(1)}, f32[8,16,128]{2,1,0:T(8,128)}, u32[]{:S(2)}) copy-start(f32[8,16,128]{2,1,0:T(8,128)} %north_c.5) | copy-start | bytes 196612
  3.4 11.8 %copy-start.4 = (f32[7,16,128]{2,1,0:T(8,128)S(1)}, f32[7,16,128]{2,1,0:T(8,128)}, u32[]{:S(2)}) copy-start(f32[7,16,128]{2,1,0:T(8,128)} %mixing.3) | copy-start | bytes 172036
  5.7 9.5 %collective-permute-start.2 = (bf16[8,32,128]{2,1,0:T(8,128)(2,1)S(1)}, bf16[8,32,128]{2,1,0:T(8,128)(2,1)S(1)}, u32[]{:S(2)}, u32[]{:S(2)}) collective-permute-start(bf16[8,32,128]{2,1,0:T(8,128)(2,1)S(1)} %get-tuple-element.22), channel_id=1, source_target_pairs={{0,8},{8,16},{16,24},{24,0},{1,9},{9,17},{17,25},{25,1},{2,10},{10... | collective-permute-start | bytes 196616 | tf_op jit(solution)/shard_map/ppermute | solution.py:282
  6.2 9.0 %collective-permute-start.3 = (bf16[8,32,128]{2,1,0:T(8,128)(2,1)S(1)}, bf16[8,32,128]{2,1,0:T(8,128)(2,1)S(1)}, u32[]{:S(2)}, u32[]{:S(2)}) collective-permute-start(bf16[8,32,128]{2,1,0:T(8,128)(2,1)S(1)} %get-tuple-element.23), channel_id=1, source_target_pairs={{8,0},{16,8},{24,16},{0,24},{9,1},{17,9},{25,17},{1,25},{10,2},{18... | collective-permute-start | bytes 196616 | tf_op jit(solution)/shard_map/ppermute | solution.py:283
  8.1 7.0 %collective-permute-start = (f32[32,128]{1,0:T(8,128)S(1)}, f32[32,128]{1,0:T(8,128)S(1)}, u32[]{:S(2)}, u32[]{:S(2)}) collective-permute-start(f32[32,128]{1,0:T(8,128)S(1)} %get-tuple-element.20), channel_id=1, source_target_pairs={{0,1},{1,2},{2,3},{3,4},{4,5},{5,6},{6,7},{7,0},{8,9},{9,10},{10,1... | collective-permute-start | bytes 49160 | tf_op jit(solution)/shard_map/ppermute | solution.py:284
  10.4 4.8 %collective-permute-start.1 = (f32[32,128]{1,0:T(8,128)S(1)}, f32[32,128]{1,0:T(8,128)S(1)}, u32[]{:S(2)}, u32[]{:S(2)}) collective-permute-start(f32[32,128]{1,0:T(8,128)S(1)} %get-tuple-element.21), channel_id=1, source_target_pairs={{1,0},{2,1},{3,2},{4,3},{5,4},{6,5},{7,6},{0,7},{9,8},{10,9},{11,1... | collective-permute-start | bytes 49160 | tf_op jit(solution)/shard_map/ppermute | solution.py:285
  33.3 8.2 %collective-permute-start.6 = (bf16[8,32,128]{2,1,0:T(8,128)(2,1)S(1)}, bf16[8,32,128]{2,1,0:T(8,128)(2,1)S(1)}, u32[]{:S(2)}, u32[]{:S(2)}) collective-permute-start(bf16[8,32,128]{2,1,0:T(8,128)(2,1)S(1)} %get-tuple-element.27), channel_id=1, source_target_pairs={{0,8},{8,16},{16,24},{24,0},{1,9},{9,17},{17,25},{25,1},{2,10},{10... | collective-permute-start | bytes 196616 | tf_op jit(solution)/shard_map/ppermute | solution.py:282
  33.4 8.2 %collective-permute-start.7 = (bf16[8,32,128]{2,1,0:T(8,128)(2,1)S(1)}, bf16[8,32,128]{2,1,0:T(8,128)(2,1)S(1)}, u32[]{:S(2)}, u32[]{:S(2)}) collective-permute-start(bf16[8,32,128]{2,1,0:T(8,128)(2,1)S(1)} %get-tuple-element.28), channel_id=1, source_target_pairs={{8,0},{16,8},{24,16},{0,24},{9,1},{17,9},{25,17},{1,25},{10,2},{18... | collective-permute-start | bytes 196616 | tf_op jit(solution)/shard_map/ppermute | solution.py:283
  35.1 6.4 %collective-permute-start.4 = (f32[32,128]{1,0:T(8,128)S(1)}, f32[32,128]{1,0:T(8,128)S(1)}, u32[]{:S(2)}, u32[]{:S(2)}) collective-permute-start(f32[32,128]{1,0:T(8,128)S(1)} %get-tuple-element.25), channel_id=1, source_target_pairs={{0,1},{1,2},{2,3},{3,4},{4,5},{5,6},{6,7},{7,0},{8,9},{9,10},{10,1... | collective-permute-start | bytes 49160 | tf_op jit(solution)/shard_map/ppermute | solution.py:284
  36.5 5.0 %collective-permute-start.5 = (f32[32,128]{1,0:T(8,128)S(1)}, f32[32,128]{1,0:T(8,128)S(1)}, u32[]{:S(2)}, u32[]{:S(2)}) collective-permute-start(f32[32,128]{1,0:T(8,128)S(1)} %get-tuple-element.26), channel_id=1, source_target_pairs={{1,0},{2,1},{3,2},{4,3},{5,4},{6,5},{7,6},{0,7},{9,8},{10,9},{11,1... | collective-permute-start | bytes 49160 | tf_op jit(solution)/shard_map/ppermute | solution.py:285
